TPU v7x, 32 devices: a whole 2x2x4 slice. The times are simulated.
32 devices in a mesh: dom: 4 (over y, core), narrow: 8 (over z, x).
Axes of the slice: x: 2, y: 2, z: 4, core: 2. Of those that a mesh axis runs over, the one named last changes fastest.
Arguments:
- feats: bfloat16 [32768, 768], P(('dom', 'narrow')), may hold values from -21 to 21
- node_type: int32 [256], P('dom'), may hold values from 0 to 2
- tiles: int32 [256, 4], P('dom'), may hold values from 0 to 63, as said below
- relation: int32 [256, 4], P(('dom', 'narrow')), may hold values from 0 to 4
- neg_sched: int32 [32, 4], P('dom'), may hold values from 0 to 7
- w_query: bfloat16 [3, 768, 768], replicated, may hold values from -0.21875 to 0.21875
- w_key: bfloat16 [3, 768, 768], replicated, may hold values from -0.21875 to 0.21875
- w_value: bfloat16 [3, 768, 768], replicated, may hold values from -0.21875 to 0.21875
- w_out: bfloat16 [3, 768, 768], replicated, may hold values from -0.21875 to 0.21875
- rel_att: bfloat16 [5, 8, 96, 96], replicated, may hold values from -0.625 to 0.625
- rel_msg: bfloat16 [5, 8, 96, 96], replicated, may hold values from -0.625 to 0.625
- rel_prior: float32 [5, 8], replicated, may hold values from 0.5 to 2
- skip_gate: float32 [3], replicated, may hold values from -2 to 2
- pos_view: bfloat16 [32768, 768], P(('dom', 'narrow')), may hold values from -6 to 6
- type_weight: float32 [3], replicated, may hold values from 0.5 to 2
Outputs:
- embedding: bfloat16 [32768, 768], P(('dom', 'narrow'))
- node_loss: float32 [32768], P(('dom', 'narrow'))
- mean_loss: float32 [], replicated
Inputs may be any that keep to these rules, and one draw needn't show every extreme that they name: `tiles`: values are block numbers within the target block's group: owner lane times 8 plus the owner's local block. Among the 32 entries of one device's target blocks, at most 5 name blocks of any one lane.
All inputs are finite; a program needn't handle non-finite values.
Results may differ from a plain program's by a relative error of at most 0.008.
The roundings to bfloat16 on the way count: a program that leaves them out, or rounds other values in their place, can miss the bound.
Values may be sent and summed in bfloat16 or wider, within the bound.
No kernel may reach another device: no remote copies, remote signals or barrier semaphores. Data moves between devices by JAX's collectives and lax.ppermute only.
A program may use at most 128 MiB of HBM per device.

v0:
```python
import math

import jax
import jax.numpy as jnp
from jax import lax
from jax.sharding import PartitionSpec as P

D = 768
HEADS = 8
DH = 96
TILE = 128
NT = 4


def shifted(array, axis, by):
    count = lax.axis_size(axis)
    return lax.ppermute(array, axis, [(i, (i + by) % count) for i in range(count)])


def shards(
    feats,
    node_type,
    tiles,
    relation,
    neg_sched,
    w_query,
    w_key,
    w_value,
    w_out,
    rel_att,
    rel_msg,
    rel_prior,
    skip_gate,
    pos_view,
    type_weight,
):
    lane_count = lax.axis_size("narrow")
    my_lane = lax.axis_index("narrow")
    nblocks = feats.shape[0] // TILE
    requests = nblocks * NT
    capacity = (requests + lane_count - 1) // lane_count + 1
    blocks = feats.reshape(nblocks, TILE, D)
    group_lists = tiles.reshape(lane_count, requests)
    owners = group_lists // nblocks
    local_tile = group_lists % nblocks
    position = jnp.arange(requests, dtype=jnp.int32)
    before = position[None, :] < position[:, None]
    same_owner = owners[:, :, None] == owners[:, None, :]
    rank_of = jnp.sum(jnp.logical_and(same_owner, before[None]).astype(jnp.int32), axis=2)
    my_tiles = lax.dynamic_index_in_dim(group_lists, my_lane, 0, keepdims=False)
    my_owners = lax.dynamic_index_in_dim(owners, my_lane, 0, keepdims=False)
    my_ranks = lax.dynamic_index_in_dim(rank_of, my_lane, 0, keepdims=False)
    own_types = lax.dynamic_slice_in_dim(node_type, my_lane * nblocks, nblocks)
    source_types = node_type[my_tiles].reshape(nblocks, NT)
    columns = blocks.shape[2]
    slot_ids = jnp.arange(capacity, dtype=jnp.int32)
    chosen = jnp.logical_and(
        (owners == my_lane)[:, :, None], rank_of[:, :, None] == slot_ids[None, None, :]
    )
    send_index = jnp.sum(chosen.astype(jnp.int32) * local_tile[:, :, None], axis=1)
    outgoing = blocks[send_index]
    incoming = lax.all_to_all(outgoing, "narrow", split_axis=0, concat_axis=0, tiled=True)
    fetched = incoming.reshape(lane_count * capacity, TILE, columns)[
        my_owners * capacity + my_ranks
    ]
    fetched = fetched.reshape(nblocks, NT, TILE, columns)

    def attend(inputs):
        own_rows, type_id, src_tiles, src_types, rel_ids = inputs
        query_rows = jnp.dot(own_rows, w_query[type_id], preferred_element_type=jnp.float32).astype(
            jnp.bfloat16
        )
        src_keys = jnp.einsum(
            "jmd,jde->jme", src_tiles, w_key[src_types], preferred_element_type=jnp.float32
        ).astype(jnp.bfloat16)
        src_values = jnp.einsum(
            "jmd,jde->jme", src_tiles, w_value[src_types], preferred_element_type=jnp.float32
        ).astype(jnp.bfloat16)
        keyed_rows = jnp.einsum(
            "jmhd,jhde->jmhe",
            src_keys.reshape(NT, TILE, HEADS, DH),
            rel_att[rel_ids],
            preferred_element_type=jnp.float32,
        ).astype(jnp.bfloat16)
        message = jnp.einsum(
            "jmhd,jhde->jmhe",
            src_values.reshape(NT, TILE, HEADS, DH),
            rel_msg[rel_ids],
            preferred_element_type=jnp.float32,
        ).astype(jnp.bfloat16)
        scores = jnp.einsum(
            "ihd,jmhd->hijm",
            query_rows.reshape(TILE, HEADS, DH),
            keyed_rows,
            preferred_element_type=jnp.float32,
        )
        prior_scale = jnp.transpose(rel_prior[rel_ids]) / math.sqrt(DH)
        scores = (scores * prior_scale[:, None, :, None]).reshape(HEADS, TILE, NT * TILE)
        highest = jnp.max(scores, axis=2, keepdims=True)
        exponent = jnp.exp(scores - highest)
        attention = (exponent / jnp.sum(exponent, axis=2, keepdims=True)).astype(jnp.bfloat16)
        merged = jnp.einsum(
            "hin,nhe->ihe",
            attention,
            message.reshape(NT * TILE, HEADS, DH),
            preferred_element_type=jnp.float32,
        )
        activated = jax.nn.gelu(merged.reshape(TILE, D), approximate=False).astype(jnp.bfloat16)
        projected = jnp.dot(activated, w_out[type_id], preferred_element_type=jnp.float32)
        mix_gate = jax.nn.sigmoid(skip_gate[type_id])
        return (mix_gate * projected + (1.0 - mix_gate) * own_rows.astype(jnp.float32)).astype(
            jnp.bfloat16
        )

    embedding_blocks = lax.map(attend, (blocks, own_types, fetched, source_types, relation))
    steps_count = lane_count // 2
    my_sched = lax.dynamic_index_in_dim(neg_sched, my_lane, 0, keepdims=False)
    gathered_negs = []
    for offset in range(1, steps_count + 1):
        chosen_block = lax.dynamic_index_in_dim(
            embedding_blocks, my_sched[offset - 1], 0, keepdims=False
        )
        gathered_negs.append(shifted(chosen_block, "narrow", offset))
    negatives = jnp.stack(gathered_negs).reshape(steps_count * TILE, D)
    offsets = jnp.arange(1, steps_count + 1, dtype=jnp.int32)
    sender_lane = (my_lane - offsets) % lane_count
    neg_blocks = neg_sched[sender_lane, offsets - 1]
    neg_types = jnp.repeat(
        node_type[sender_lane * nblocks + neg_blocks], TILE, total_repeat_length=steps_count * TILE
    )
    row_types = jnp.repeat(own_types, TILE, total_repeat_length=nblocks * TILE)
    embedding = embedding_blocks.reshape(nblocks * TILE, D)
    positive = jnp.einsum(
        "nd,nd->n", embedding, pos_view, preferred_element_type=jnp.float32
    ) / math.sqrt(D)
    neg_logits = jnp.einsum(
        "nd,md->nm", embedding, negatives, preferred_element_type=jnp.float32
    ) / math.sqrt(D)
    neg_logits = jnp.where(row_types[:, None] == neg_types[None, :], neg_logits, -jnp.inf)
    highest = jnp.maximum(positive, jnp.max(neg_logits, axis=1))
    denominator = jnp.exp(positive - highest) + jnp.sum(
        jnp.exp(neg_logits - highest[:, None]), axis=1
    )
    node_loss = highest + jnp.log(denominator) - positive
    type_match = (
        row_types[:, None] == jnp.arange(type_weight.shape[0], dtype=jnp.int32)[None, :]
    ).astype(jnp.float32)
    row_weight = jnp.sum(type_match * type_weight[None, :], axis=1)
    overall = lax.psum(jnp.sum(row_weight * node_loss), ("dom", "narrow"))
    mean_loss = overall / (node_loss.shape[0] * lax.axis_size("dom") * lax.axis_size("narrow"))
    return (embedding, node_loss, mean_loss)


def solution(mesh):
    return jax.shard_map(
        shards,
        mesh=mesh,
        in_specs=(
            P(("dom", "narrow"), None),
            P("dom"),
            P("dom", None),
            P(("dom", "narrow"), None),
            P("dom", None),
            P(),
            P(),
            P(),
            P(),
            P(),
            P(),
            P(),
            P(),
            P(("dom", "narrow"), None),
            P(),
        ),
        out_specs=(P(("dom", "narrow"), None), P(("dom", "narrow")), P()),
        check_vma=False,
    )
```

profile of v0, /device:TPU:12, one launch (start us, length us, event | category | flops | bytes accessed | tf_op | source)
XLA Modules:
  0.0 586.4 jit_solution(2435087327555818215)
XLA Ops:
  2.2 7.3 %gather_fusion.5 = bf16[40,128,768]{2,1,0:T(8,128)(2,1)} fusion(bf16[8,128,768]{2,1,0:T(8,128)(2,1)} %bitcast.282, s32[1024]{0:T(1024)S(1)} %pad_clamp_fusion.5), kind=kCustom, calls=%fused_computation.5 | custom fusion | bytes 15728800 | tf_op jit(solution)/shard_map/gather | solution.py:61
  9.5 6.4 %all-to-all-start = ((bf16[8,5,128,768]{3,2,1,0:T(8,128)(2,1)}), bf16[8,5,128,768]{3,2,1,0:T(8,128)(2,1)}, u32[]{:S(2)}, u32[]{:S(2)}) async-start(bf16[8,5,128,768]{3,2,1,0:T(8,128)(2,1)} %bitcast.285), calls=%async_computation | async-start | bytes 15728640 | tf_op jit(solution)/shard_map/all_to_all | solution.py:62
  30.3 4.2 compare_select_fusion.3
  35.9 2.5 compare_select_fusion.12
  39.0 146.3 %all-to-all-done = bf16[8,5,128,768]{3,2,1,0:T(8,128)(2,1)} async-done(((bf16[8,5,128,768]{3,2,1,0:T(8,128)(2,1)}), bf16[8,5,128,768]{3,2,1,0:T(8,128)(2,1)}, u32[]{:S(2)}, u32[]{:S(2)}) %all-to-all-start) | async-done | bytes 7864352 | tf_op jit(solution)/shard_map/all_to_all | solution.py:62
  185.3 7.1 %gather_fusion.6 = bf16[32,128,768]{2,1,0:T(8,128)(2,1)} fusion(bf16[40,128,768]{2,1,0:T(8,128)(2,1)} %bitcast.27, s32[1024]{0:T(1024)S(1)} %pad_clamp_fusion.4), kind=kCustom, calls=%fused_computation.6 | custom fusion | bytes 12583040 | tf_op jit(solution)/shard_map/gather | solution.py:63
  192.3 317.1 %while.12 = (s32[]{:T(128)}, bf16[8,128,768]{2,1,0:T(8,128)(2,1)}, s32[8]{0:T(128)}, f32[3]{0:T(128)}, s32[8,4]{1,0:T(8,128)}, /*index=5*/bf16[5,8,96,96]{3,2,1,...) while((s32[]{:T(128)}, bf16[8,128,768]{2,1,0:T(8,128)(2,1)}, ...), condition=%wide.region_5.6_spmd, body=%wide.region_2.5_spmd.sunk | while | flops 1874493440 | bytes 85165208 | solution.py:115
  195.5 2.4 fusion.132
  200.3 3.0 gather_fusion.2
  203.3 3.4 convolution_convert_fusion.6
  214.2 5.0 gather_fusion.4
  219.2 3.4 convolution_convert_fusion.7
  240.0 3.0 gather_fusion.2
  242.9 3.4 convolution_convert_fusion.6
  253.9 5.0 gather_fusion.4
  258.8 3.4 convolution_convert_fusion.7
  274.8 2.4 fusion.132
  279.6 3.0 gather_fusion.2
  282.6 3.4 convolution_convert_fusion.6
  293.5 5.0 gather_fusion.4
  298.5 3.4 convolution_convert_fusion.7
  314.4 2.4 fusion.132
  319.2 3.0 gather_fusion.2
  322.2 3.4 convolution_convert_fusion.6
  333.1 5.0 gather_fusion.4
  338.1 3.4 convolution_convert_fusion.7
  354.0 2.4 fusion.132
  358.9 3.0 gather_fusion.2
  361.9 3.4 convolution_convert_fusion.6
  372.8 5.0 gather_fusion.4
  377.7 3.4 convolution_convert_fusion.7
  393.7 2.4 fusion.132
  398.5 3.0 gather_fusion.2
  401.5 3.4 convolution_convert_fusion.6
  412.4 5.0 gather_fusion.4
  417.4 3.4 convolution_convert_fusion.7
  433.3 2.4 fusion.132
  438.2 3.0 gather_fusion.2
  441.1 3.4 convolution_convert_fusion.6
  452.0 5.0 gather_fusion.4
  457.0 3.4 convolution_convert_fusion.7
  477.8 3.0 gather_fusion.2
  480.8 3.4 convolution_convert_fusion.6
  491.7 5.0 gather_fusion.4
  496.7 3.4 convolution_convert_fusion.7
  513.0 4.3 collective-permute-start.2
  520.2 10.6 %collective-permute-done.2 = bf16[128,768]{1,0:T(8,128)(2,1)S(1)} collective-permute-done((bf16[128,768]{1,0:T(8,128)(2,1)S(1)}, bf16[128,768]{1,0:T(8,128)(2,1)S(1)}, u32[]{:S(2)}, u32[]{:S(2)}) %collective-permute-start.2) | collective-permute-done | bytes 196640 | tf_op jit(solution)/shard_map/ppermute | solution.py:17
  533.9 50.8 %psum.7 = f32[]{:T(128)} all-reduce(f32[]{:T(128)} %get-tuple-element.180), channel_id=1, replica_groups=mesh['dom'=4,'narrow'=8] {'dom','narrow'}, use_global_device_ids=true, to_apply=%region_10.11 | all-reduce | flops 1 | bytes 8 | tf_op jit(solution)/shard_map/psum | solution.py:149
  (356 shorter events, 183.3 us)
Async XLA Ops:
  0.6 15.3 %copy-start = (s32[8,4]{0,1:T(4,128)S(1)}, s32[8,4]{0,1:T(4,128)}, u32[]{:S(2)}) copy-start(s32[8,4]{0,1:T(4,128)} %param.25) | copy-start | bytes 388
  9.5 12.3 %copy-start.2 = (s32[64]{0:T(128)S(1)}, s32[64]{0:T(128)}, u32[]{:S(2)}) copy-start(s32[64]{0:T(128)} %param.22) | copy-start | bytes 772
  9.5 13.8 %copy-start.17 = (s32[8,4]{0,1:T(4,128)S(1)}, s32[8,4]{0,1:T(4,128)}, u32[]{:S(2)}) copy-start(s32[8,4]{0,1:T(4,128)} %param.24) | copy-start | bytes 388
  9.5 25.7 %copy-start.18 = (f32[3]{0:T(128)S(1)}, f32[3]{0:T(128)}, u32[]{:S(2)}) copy-start(f32[3]{0:T(128)} %param.35) | copy-start | bytes 40
  9.5 175.8 %all-to-all-start = ((bf16[8,5,128,768]{3,2,1,0:T(8,128)(2,1)}), bf16[8,5,128,768]{3,2,1,0:T(8,128)(2,1)}, u32[]{:S(2)}, u32[]{:S(2)}) async-start(bf16[8,5,128,768]{3,2,1,0:T(8,128)(2,1)} %bitcast.285), calls=%async_computation | async-start | bytes 15728640 | tf_op jit(solution)/shard_map/all_to_all | solution.py:62
  35.2 150.1 %copy-start.11 = (s32[1024]{0:T(1024)}, s32[1024]{0:T(1024)S(1)}, u32[]{:S(2)}) copy-start(s32[1024]{0:T(1024)S(1)} %select_select_fusion) | copy-start | bytes 12292
  185.3 7.1 %copy-start.3 = (bf16[3,768,768]{2,1,0:T(8,128)(2,1)S(1)}, bf16[3,768,768]{2,1,0:T(8,128)(2,1)}, u32[]{:S(2)}) copy-start(bf16[3,768,768]{2,1,0:T(8,128)(2,1)} %param.27) | copy-start | bytes 10616836
  185.3 7.1 %copy-start.10 = (f32[5,8]{1,0:T(8,128)S(1)}, f32[5,8]{1,0:T(8,128)}, u32[]{:S(2)}) copy-start(f32[5,8]{1,0:T(8,128)} %param.32) | copy-start | bytes 484
  192.3 8.0 %copy-start.14 = (s32[8,4]{1,0:T(8,128)}, s32[8,4]{1,0:T(8,128)S(1)}, u32[]{:S(2)}) copy-start(s32[8,4]{1,0:T(8,128)S(1)} %get-tuple-element.356) | copy-start | bytes 388 | tf_op jit(solution)/shard_map/while
  206.7 3.4 copy-start.6
  226.1 5.9 %copy-start.4 = (bf16[3,768,768]{2,1,0:T(8,128)(2,1)S(1)}, bf16[3,768,768]{2,1,0:T(8,128)(2,1)}, u32[]{:S(2)}) copy-start(bf16[3,768,768]{2,1,0:T(8,128)(2,1)} %get-tuple-element.389) | copy-start | bytes 10616836 | tf_op jit(solution)/shard_map/while
  226.1 5.9 %copy-start.15 = (s32[8,4]{1,0:T(8,128)S(1)}, s32[8,4]{1,0:T(8,128)}, u32[]{:S(2)}) copy-start(s32[8,4]{1,0:T(8,128)} %copy-done.14) | copy-start | bytes 388 | tf_op jit(solution)/shard_map/while
  232.0 8.0 %copy-start.14 = (s32[8,4]{1,0:T(8,128)}, s32[8,4]{1,0:T(8,128)S(1)}, u32[]{:S(2)}) copy-start(s32[8,4]{1,0:T(8,128)S(1)} %get-tuple-element.356) | copy-start | bytes 388 | tf_op jit(solution)/shard_map/while
  246.3 3.4 copy-start.6
  265.7 5.9 %copy-start.4 = (bf16[3,768,768]{2,1,0:T(8,128)(2,1)S(1)}, bf16[3,768,768]{2,1,0:T(8,128)(2,1)}, u32[]{:S(2)}) copy-start(bf16[3,768,768]{2,1,0:T(8,128)(2,1)} %get-tuple-element.389) | copy-start | bytes 10616836 | tf_op jit(solution)/shard_map/while
  265.7 5.9 %copy-start.15 = (s32[8,4]{1,0:T(8,128)S(1)}, s32[8,4]{1,0:T(8,128)}, u32[]{:S(2)}) copy-start(s32[8,4]{1,0:T(8,128)} %copy-done.14) | copy-start | bytes 388 | tf_op jit(solution)/shard_map/while
  271.6 8.0 %copy-start.14 = (s32[8,4]{1,0:T(8,128)}, s32[8,4]{1,0:T(8,128)S(1)}, u32[]{:S(2)}) copy-start(s32[8,4]{1,0:T(8,128)S(1)} %get-tuple-element.356) | copy-start | bytes 388 | tf_op jit(solution)/shard_map/while
  286.0 3.4 copy-start.6
  305.3 5.9 %copy-start.4 = (bf16[3,768,768]{2,1,0:T(8,128)(2,1)S(1)}, bf16[3,768,768]{2,1,0:T(8,128)(2,1)}, u32[]{:S(2)}) copy-start(bf16[3,768,768]{2,1,0:T(8,128)(2,1)} %get-tuple-element.389) | copy-start | bytes 10616836 | tf_op jit(solution)/shard_map/while
  305.3 5.9 %copy-start.15 = (s32[8,4]{1,0:T(8,128)S(1)}, s32[8,4]{1,0:T(8,128)}, u32[]{:S(2)}) copy-start(s32[8,4]{1,0:T(8,128)} %copy-done.14) | copy-start | bytes 388 | tf_op jit(solution)/shard_map/while
  311.3 8.0 %copy-start.14 = (s32[8,4]{1,0:T(8,128)}, s32[8,4]{1,0:T(8,128)S(1)}, u32[]{:S(2)}) copy-start(s32[8,4]{1,0:T(8,128)S(1)} %get-tuple-element.356) | copy-start | bytes 388 | tf_op jit(solution)/shard_map/while
  325.6 3.4 copy-start.6
  345.0 5.9 %copy-start.4 = (bf16[3,768,768]{2,1,0:T(8,128)(2,1)S(1)}, bf16[3,768,768]{2,1,0:T(8,128)(2,1)}, u32[]{:S(2)}) copy-start(bf16[3,768,768]{2,1,0:T(8,128)(2,1)} %get-tuple-element.389) | copy-start | bytes 10616836 | tf_op jit(solution)/shard_map/while
  345.0 5.9 %copy-start.15 = (s32[8,4]{1,0:T(8,128)S(1)}, s32[8,4]{1,0:T(8,128)}, u32[]{:S(2)}) copy-start(s32[8,4]{1,0:T(8,128)} %copy-done.14) | copy-start | bytes 388 | tf_op jit(solution)/shard_map/while
  350.9 8.0 %copy-start.14 = (s32[8,4]{1,0:T(8,128)}, s32[8,4]{1,0:T(8,128)S(1)}, u32[]{:S(2)}) copy-start(s32[8,4]{1,0:T(8,128)S(1)} %get-tuple-element.356) | copy-start | bytes 388 | tf_op jit(solution)/shard_map/while
  365.2 3.4 copy-start.6
  384.6 5.9 %copy-start.4 = (bf16[3,768,768]{2,1,0:T(8,128)(2,1)S(1)}, bf16[3,768,768]{2,1,0:T(8,128)(2,1)}, u32[]{:S(2)}) copy-start(bf16[3,768,768]{2,1,0:T(8,128)(2,1)} %get-tuple-element.389) | copy-start | bytes 10616836 | tf_op jit(solution)/shard_map/while
  384.6 5.9 %copy-start.15 = (s32[8,4]{1,0:T(8,128)S(1)}, s32[8,4]{1,0:T(8,128)}, u32[]{:S(2)}) copy-start(s32[8,4]{1,0:T(8,128)} %copy-done.14) | copy-start | bytes 388 | tf_op jit(solution)/shard_map/while
  390.5 8.0 %copy-start.14 = (s32[8,4]{1,0:T(8,128)}, s32[8,4]{1,0:T(8,128)S(1)}, u32[]{:S(2)}) copy-start(s32[8,4]{1,0:T(8,128)S(1)} %get-tuple-element.356) | copy-start | bytes 388 | tf_op jit(solution)/shard_map/while
  404.9 3.4 copy-start.6
  424.3 5.9 %copy-start.4 = (bf16[3,768,768]{2,1,0:T(8,128)(2,1)S(1)}, bf16[3,768,768]{2,1,0:T(8,128)(2,1)}, u32[]{:S(2)}) copy-start(bf16[3,768,768]{2,1,0:T(8,128)(2,1)} %get-tuple-element.389) | copy-start | bytes 10616836 | tf_op jit(solution)/shard_map/while
  424.3 5.9 %copy-start.15 = (s32[8,4]{1,0:T(8,128)S(1)}, s32[8,4]{1,0:T(8,128)}, u32[]{:S(2)}) copy-start(s32[8,4]{1,0:T(8,128)} %copy-done.14) | copy-start | bytes 388 | tf_op jit(solution)/shard_map/while
  430.2 8.0 %copy-start.14 = (s32[8,4]{1,0:T(8,128)}, s32[8,4]{1,0:T(8,128)S(1)}, u32[]{:S(2)}) copy-start(s32[8,4]{1,0:T(8,128)S(1)} %get-tuple-element.356) | copy-start | bytes 388 | tf_op jit(solution)/shard_map/while
  444.5 3.4 copy-start.6
  463.9 5.9 %copy-start.4 = (bf16[3,768,768]{2,1,0:T(8,128)(2,1)S(1)}, bf16[3,768,768]{2,1,0:T(8,128)(2,1)}, u32[]{:S(2)}) copy-start(bf16[3,768,768]{2,1,0:T(8,128)(2,1)} %get-tuple-element.389) | copy-start | bytes 10616836 | tf_op jit(solution)/shard_map/while
  463.9 5.9 %copy-start.15 = (s32[8,4]{1,0:T(8,128)S(1)}, s32[8,4]{1,0:T(8,128)}, u32[]{:S(2)}) copy-start(s32[8,4]{1,0:T(8,128)} %copy-done.14) | copy-start | bytes 388 | tf_op jit(solution)/shard_map/while
  469.8 8.0 %copy-start.14 = (s32[8,4]{1,0:T(8,128)}, s32[8,4]{1,0:T(8,128)S(1)}, u32[]{:S(2)}) copy-start(s32[8,4]{1,0:T(8,128)S(1)} %get-tuple-element.356) | copy-start | bytes 388 | tf_op jit(solution)/shard_map/while
  484.2 3.4 copy-start.6
  503.5 5.9 %copy-start.4 = (bf16[3,768,768]{2,1,0:T(8,128)(2,1)S(1)}, bf16[3,768,768]{2,1,0:T(8,128)(2,1)}, u32[]{:S(2)}) copy-start(bf16[3,768,768]{2,1,0:T(8,128)(2,1)} %get-tuple-element.389) | copy-start | bytes 10616836 | tf_op jit(solution)/shard_map/while
  503.5 5.9 %copy-start.15 = (s32[8,4]{1,0:T(8,128)S(1)}, s32[8,4]{1,0:T(8,128)}, u32[]{:S(2)}) copy-start(s32[8,4]{1,0:T(8,128)} %copy-done.14) | copy-start | bytes 388 | tf_op jit(solution)/shard_map/while
  509.5 7.9 %copy-start.9 = (bf16[8,128,768]{2,1,0:T(8,128)(2,1)S(1)}, bf16[8,128,768]{2,1,0:T(8,128)(2,1)}, u32[]{:S(2)}) copy-start(bf16[8,128,768]{2,1,0:T(8,128)(2,1)} %get-tuple-element.370) | copy-start | bytes 4718596
  510.8 9.3 %collective-permute-start = (bf16[128,768]{1,0:T(8,128)(2,1)S(1)}, bf16[128,768]{1,0:T(8,128)(2,1)S(1)}, u32[]{:S(2)}, u32[]{:S(2)}) collective-permute-start(bf16[128,768]{1,0:T(8,128)(2,1)S(1)} %get-tuple-element.188), channel_id=1, source_target_pairs={{0,1},{1,2},{2,3},{3,4},{4,5},{5,6},{6,7},{7,0},{8,9},{9,10},{10,1... | collective-permute-start | bytes 589832 | tf_op jit(solution)/shard_map/ppermute | solution.py:17
  511.5 8.6 %collective-permute-start.1 = (bf16[128,768]{1,0:T(8,128)(2,1)S(1)}, bf16[128,768]{1,0:T(8,128)(2,1)S(1)}, u32[]{:S(2)}, u32[]{:S(2)}) collective-permute-start(bf16[128,768]{1,0:T(8,128)(2,1)S(1)} %get-tuple-element.191), channel_id=1, source_target_pairs={{0,2},{1,3},{2,4},{3,5},{4,6},{5,7},{6,0},{7,1},{8,10},{9,11},{10,... | collective-permute-start | bytes 589832 | tf_op jit(solution)/shard_map/ppermute | solution.py:17
  513.0 17.8 %collective-permute-start.2 = (bf16[128,768]{1,0:T(8,128)(2,1)S(1)}, bf16[128,768]{1,0:T(8,128)(2,1)S(1)}, u32[]{:S(2)}, u32[]{:S(2)}) collective-permute-start(bf16[128,768]{1,0:T(8,128)(2,1)S(1)} %get-tuple-element.190), channel_id=1, source_target_pairs={{0,3},{1,4},{2,5},{3,6},{4,7},{5,0},{6,1},{7,2},{8,11},{9,12},{10,... | collective-permute-start | bytes 589832 | tf_op jit(solution)/shard_map/ppermute | solution.py:17
  517.3 13.6 %copy-start.12 = (s32[1024]{0:T(1024)S(1)}, s32[1024]{0:T(1024)}, u32[]{:S(2)}) copy-start(s32[1024]{0:T(1024)} %copy-done.11) | copy-start | bytes 12292
  517.3 13.6 %copy-start.16 = (s32[512]{0:T(512)S(1)}, s32[512]{0:T(512)}, u32[]{:S(2)}) copy-start(s32[512]{0:T(512)} %and_select_fusion.1) | copy-start | bytes 6148
  517.3 13.5 %collective-permute-start.3 = (bf16[128,768]{1,0:T(8,128)(2,1)S(1)}, bf16[128,768]{1,0:T(8,128)(2,1)S(1)}, u32[]{:S(2)}, u32[]{:S(2)}) collective-permute-start(bf16[128,768]{1,0:T(8,128)(2,1)S(1)} %get-tuple-element.189), channel_id=1, source_target_pairs={{0,4},{1,5},{2,6},{3,7},{4,0},{5,1},{6,2},{7,3},{8,12},{9,13},{10,... | collective-permute-start | bytes 589832 | tf_op jit(solution)/shard_map/ppermute | solution.py:17
  530.9 54.4 %copy-start.1 = (s32[8,4]{0,1:T(4,128)S(1)}, s32[8,4]{0,1:T(4,128)}, u32[]{:S(2)}) copy-start(s32[8,4]{0,1:T(4,128)} %param.25) | copy-start | bytes 388
  (33 other events, 50.6 us)
where the time goes:
time: 590 us; the launch traced here: 586 us
  local copies, waits for them, and re-layouts  182 us (31%)
  waiting for transfers between devices  158 us (27%)
  matrix products  130 us (22%)
  blocking collectives  50.8 us (9%)
  loops' own time  21.4 us (4%)
  other arithmetic  21.1 us (4%)
  starting transfers between devices  12.9 us (2%)
  between operations  10.4 us (2%)
    all_to_all x1, waiting for transfers between devices, shards(): lax.all_to_all(outgoing, 'narrow', split_axis=0, concat_axis=0, tiled=True)  146 us
    psum x1, blocking collectives, shards(): overall = lax.psum(jnp.sum(row_weight * node_loss), ('dom', 'narrow'))  50.8 us
    gather x8, local copies, waits for them, and re-layouts, attend(): w_value[src_types]  39.8 us
    dot_general x8, matrix products, attend(): jnp.einsum('jmd,jde->jme', src_tiles, w_key[src_types], preferred_element...  27 us
    dot_general x8, matrix products, attend(): jnp.einsum('jmd,jde->jme', src_tiles, w_value[src_types], preferred_eleme...  27 us
    gather x8, local copies, waits for them, and re-layouts, attend(): w_key[src_types]  23.8 us
    while x128, local copies, waits for them, and re-layouts  22.1 us
    another operation x1, loops' own time, shards(): lax.map(attend, (blocks, own_types, fetched, source_types, relation))  21.4 us
  transfers between devices with their start and end apart: 5, of which 3 were waited for; matrix products, arithmetic and copies ran while one was open for 3% of the time, Pallas kernels for 0%

commit v1 on v0

v1 whole, which is shorter than its diff:
```python
import functools
import math

import jax
import jax.numpy as jnp
from jax import lax
from jax.experimental import pallas as pl
from jax.experimental.pallas import tpu as pltpu
from jax.sharding import PartitionSpec as P

TILE = 128
LANES = 128
MXU = 256
F32 = jnp.float32
BF16 = jnp.bfloat16
VMEM_LIMIT = 48 * 1024 * 1024

OWN, PARTNER, BELOW, ABOVE, BELOW_X, ABOVE_X, FAR_UP, FAR_DOWN, FAR_X, ENDS, ENDS_X = range(11)
PHASES = 4


def params(cost=None):
    return dict(
        compiler_params=pltpu.CompilerParams(vmem_limit_bytes=VMEM_LIMIT),
        cost_estimate=cost,
    )


def cost(flops, nbytes, trans=0):
    return pl.CostEstimate(flops=int(flops), bytes_accessed=int(nbytes), transcendentals=int(trans))


class Layout:
    def __init__(self, lanes, nblocks, slots, steps, types):
        self.lanes, self.nblocks, self.slots, self.steps, self.types = (
            lanes, nblocks, slots, steps, types,
        )
        self.requests = nblocks * slots
        self.cap = (self.requests + lanes - 1) // lanes + 1
        at = 0
        for name, size in (
            ("partner", lanes * self.cap),
            ("ends", lanes * self.cap),
            ("ends_x", lanes * self.cap),
            ("start", PHASES + 1),
            ("slot", self.requests),
            ("buf", self.requests),
            ("idx", self.requests),
            ("kind", self.requests),
            ("rel", self.requests),
            ("qblk", nblocks),
            ("qkind", nblocks),
            ("own_kind", nblocks),
            ("offer", nblocks),
            ("sched", steps),
            ("neg_kind", steps),
            ("lane", 1),
        ):
            setattr(self, name, at)
            at += size
        self.size = at


def plan_body(lay, staged, lane_ref, tiles, kinds, relation, sched, out, count, keys, bufs, idxs):
    lanes, nblocks, slots, steps, types = lay.lanes, lay.nblocks, lay.slots, lay.steps, lay.types
    cap, requests = lay.cap, lay.requests
    lane = lane_ref[0]
    depth, side = lane // 2, lax.rem(lane, 2)

    def clear(ref, base, size):
        def one(i, _):
            ref[base + i] = 0
            return 0

        lax.fori_loop(0, size, one, 0)

    def lists_of(device, base):
        clear(count, 0, lanes)
        clear(out, base, lanes * cap)

        def one(i, _):
            tile = tiles[device * nblocks + i // slots, lax.rem(i, slots)]
            owner = tile // nblocks
            rank = count[owner]
            out[base + owner * cap + rank] = lax.rem(tile, nblocks)
            count[owner] = rank + 1
            return 0

        lax.fori_loop(0, requests, one, 0)

    out[lay.lane] = lane
    if staged:
        far = lanes // 2 - 1 - depth
        lists_of(lane + 1 - 2 * side, lay.partner)
        lists_of(far * 2 + side, lay.ends)
        lists_of(far * 2 + 1 - side, lay.ends_x)

    clear(count, 0, lanes)
    clear(keys, 0, PHASES * types)

    def place(i, _):
        tile = tiles[lane * nblocks + i // slots, lax.rem(i, slots)]
        kind = kinds[tile]
        if staged:
            owner, local = tile // nblocks, lax.rem(tile, nblocks)
            rank = count[owner]
            count[owner] = rank + 1
            delta = owner // 2 - depth
            same = lax.rem(owner, 2) == side
            away = jnp.abs(delta)
            near = jnp.where(
                same,
                jnp.where(delta > 0, ABOVE, BELOW),
                jnp.where(delta > 0, ABOVE_X, BELOW_X),
            )
            buf = jnp.where(
                away == 0,
                jnp.where(same, OWN, PARTNER),
                jnp.where(
                    away == 1,
                    near,
                    jnp.where(
                        away == 2,
                        jnp.where(same, jnp.where(delta > 0, FAR_DOWN, FAR_UP), FAR_X),
                        jnp.where(same, ENDS, ENDS_X),
                    ),
                ),
            )
            whole = jnp.logical_and(same, away <= 2)
            idx = jnp.where(whole, local, rank)
            late = jnp.where(
                away == 0,
                0,
                jnp.where(
                    away == 1,
                    jnp.where(same, 0, 1),
                    jnp.where(away == 2, jnp.where(same, 1, 2), 3),
                ),
            )
        else:
            buf, idx, late = jnp.int32(OWN), tile, jnp.int32(0)
        key = late * types + kind
        bufs[i] = buf
        idxs[i] = idx
        bufs[requests + i] = key
        bufs[2 * requests + i] = kind
        keys[key] = keys[key] + 1
        return 0

    lax.fori_loop(0, requests, place, 0)

    total = jnp.int32(0)
    for phase in range(PHASES):
        out[lay.start + phase] = total
        for kind in range(types):
            key = phase * types + kind
            size = keys[key]
            keys[key] = total
            total = total + size
    out[lay.start + PHASES] = total

    def order(i, _):
        key = bufs[requests + i]
        at = keys[key]
        keys[key] = at + 1
        out[lay.slot + at] = i
        out[lay.buf + at] = bufs[i]
        out[lay.idx + at] = idxs[i]
        out[lay.kind + at] = bufs[2 * requests + i]
        out[lay.rel + at] = relation[i // slots, lax.rem(i, slots)]
        return 0

    lax.fori_loop(0, requests, order, 0)

    at = jnp.int32(0)
    for kind in range(types):
        for block in range(nblocks):
            mine = kinds[lane * nblocks + block]
            hit = mine == kind

            @pl.when(hit)
            def _(at=at, block=block, kind=kind):
                out[lay.qblk + at] = block
                out[lay.qkind + at] = kind

            at = at + hit.astype(jnp.int32)
    for block in range(nblocks):
        out[lay.own_kind + block] = kinds[lane * nblocks + block]
        out[lay.offer + block] = -1
    for step in range(steps):
        block = sched[lane, step]
        out[lay.sched + step] = block
        out[lay.offer + block] = step
        sender = lax.rem(lane - (step + 1) + lanes, lanes)
        out[lay.neg_kind + step] = kinds[sender * nblocks + sched[sender, step]]


def make_plan(lay, staged, lane, tiles, kinds, relation, sched):
    smem = pl.BlockSpec(memory_space=pltpu.SMEM)
    return pl.pallas_call(
        functools.partial(plan_body, lay, staged),
        out_shape=jax.ShapeDtypeStruct((lay.size,), jnp.int32),
        in_specs=[smem] * 5,
        out_specs=smem,
        scratch_shapes=[
            pltpu.SMEM((lay.lanes,), jnp.int32),
            pltpu.SMEM((PHASES * lay.types,), jnp.int32),
            pltpu.SMEM((3 * lay.requests,), jnp.int32),
            pltpu.SMEM((lay.requests,), jnp.int32),
        ],
        cost_estimate=cost(1e5, 4096),
        name="plan",
    )(lane, tiles, kinds, relation, sched)


class Heads:
    def __init__(self, heads, size, width):
        self.heads, self.size, self.width = heads, size, width
        self.padded = heads * LANES
        self.pieces = []
        self.spots = []
        row = 0
        for pair in range(heads // 2):
            first = pair * 2 * size
            low = first // MXU * MXU
            high = min(-(-(first + 2 * size) // MXU) * MXU, width)
            self.pieces.append((row, low, high - low, pair * 2 * LANES))
            for half in range(2):
                self.spots.append((row + first + half * size - low, half * LANES))
            row += high - low
        self.rows = row

    def apply(self, rows, matrix, out):
        for at, low, columns, to in self.pieces:
            out[0, :, to : to + 2 * LANES] = jnp.dot(
                rows[:, low : low + columns],
                matrix[0, at : at + columns, :],
                preferred_element_type=F32,
            ).astype(BF16)


def spread_body(hd, att, msg, out_att, out_msg):
    last = pl.program_id(0) == pl.num_programs(0) - 1
    rows = lax.broadcasted_iota(jnp.int32, (hd.size, hd.size), 0)
    columns = lax.broadcasted_iota(jnp.int32, (hd.size, hd.size), 1)
    eye = (rows == columns).astype(BF16)
    for src, out in ((att, out_att), (msg, out_msg)):
        out[...] = jnp.zeros_like(out)
        for head, (row, column) in enumerate(hd.spots):
            out[0, row : row + hd.size, column : column + hd.size] = jnp.where(
                last, eye, src[0, head]
            )


def spread(hd, att, msg):
    count = att.shape[0]
    source = pl.BlockSpec(
        (1,) + att.shape[1:], lambda i: (jnp.minimum(i, count - 1), 0, 0, 0)
    )
    target = pl.BlockSpec((1, hd.rows, 2 * LANES), lambda i: (i, 0, 0))
    shape = jax.ShapeDtypeStruct((count + 1, hd.rows, 2 * LANES), BF16)
    return pl.pallas_call(
        functools.partial(spread_body, hd),
        grid=(count + 1,),
        in_specs=[source, source],
        out_specs=[target, target],
        out_shape=[shape, shape],
        name="spread",
        **params(cost(1e6, 4 * (count + 1) * hd.rows * 2 * LANES)),
    )(att, msg)


def query_body(lay, hd, plan, rows, weight, pieces, out):
    held = jnp.dot(rows[0], weight[0], preferred_element_type=F32).astype(BF16)
    hd.apply(held, pieces, out)


def queries(lay, hd, plan, blocks, weight, pieces):
    width = blocks.shape[2]
    identity = pieces.shape[0] - 1
    return pl.pallas_call(
        functools.partial(query_body, lay, hd),
        grid_spec=pltpu.PrefetchScalarGridSpec(
            num_scalar_prefetch=1,
            grid=(lay.nblocks,),
            in_specs=[
                pl.BlockSpec((1, TILE, width), lambda i, plan: (plan[lay.qblk + i], 0, 0)),
                pl.BlockSpec((1, width, width), lambda i, plan: (plan[lay.qkind + i], 0, 0)),
                pl.BlockSpec((1, hd.rows, 2 * LANES), lambda i, plan: (identity, 0, 0)),
            ],
            out_specs=pl.BlockSpec(
                (1, TILE, hd.padded), lambda i, plan: (plan[lay.qblk + i], 0, 0)
            ),
        ),
        out_shape=jax.ShapeDtypeStruct((lay.nblocks, TILE, hd.padded), BF16),
        name="queries",
        **params(cost(2e9, 10e6)),
    )(plan, blocks, weight, pieces)


def pick_body(wanted, nbufs, plan, *refs):
    sources, outs, sem = refs[:nbufs], refs[nbufs:-1], refs[-1]
    copies = []
    for out, (choose, cap) in zip(outs, wanted):
        for k in range(cap):
            copies.append(choose(plan, sources, out.at[k], k, sem.at[len(copies)]))
    for wait in copies:
        wait()


def pick(lay, plan, sources, wanted):
    def chooser(base_of, source_of):
        def choose(plan_ref, refs, target, k, sem):
            block = plan_ref[base_of(plan_ref) + k]
            source_of(plan_ref, refs, block, target, sem)
            return lambda: pltpu.make_async_copy(refs[0].at[0], target, sem).wait()

        return choose

    shape = sources[0].shape[1:]
    anywhere = pl.BlockSpec(memory_space=pl.ANY)
    count = len(wanted) * lay.cap
    return pl.pallas_call(
        functools.partial(
            pick_body, [(chooser(b, s), lay.cap) for b, s in wanted], len(sources)
        ),
        grid_spec=pltpu.PrefetchScalarGridSpec(
            num_scalar_prefetch=1,
            grid=(),
            in_specs=[anywhere] * len(sources),
            out_specs=[anywhere] * len(wanted),
            scratch_shapes=[pltpu.SemaphoreType.DMA((count,))],
        ),
        out_shape=[jax.ShapeDtypeStruct((lay.cap,) + shape, BF16)] * len(wanted),
        name="pick",
        **params(cost(1e3, count * 4 * shape[0] * shape[1])),
    )(plan, *sources)


def source_body(lay, hd, phase, codes, plan, *refs):
    nbufs = len(codes)
    bufs = refs[:nbufs]
    w_key, w_value, p_att, p_msg = refs[nbufs : nbufs + 4]
    keyed, message, held, sem = refs[-4:]
    step = pl.program_id(0)
    start = plan[lay.start + phase]
    count = plan[lay.start + phase + 1] - start

    def fetch(at):
        into = lax.rem(at, 2)
        which, block = plan[lay.buf + start + at], plan[lay.idx + start + at]
        for code, ref in zip(codes, bufs):

            @pl.when(which == code)
            def _(ref=ref):
                pltpu.make_async_copy(ref.at[block], held.at[into], sem.at[into]).start()

    @pl.when(jnp.logical_and(step == 0, count > 0))
    def _():
        fetch(0)

    @pl.when(step + 1 < count)
    def _():
        fetch(step + 1)

    @pl.when(step < count)
    def _():
        now = lax.rem(step, 2)
        pltpu.make_async_copy(bufs[0].at[0], held.at[now], sem.at[now]).wait()
        rows = held[now]
        key = jnp.dot(rows, w_key[0], preferred_element_type=F32).astype(BF16)
        hd.apply(key, p_att, keyed)
        value = jnp.dot(rows, w_value[0], preferred_element_type=F32).astype(BF16)
        hd.apply(value, p_msg, message)


def sources_of(lay, hd, plan, phase, most, bufs, w_key, w_value, p_att, p_msg, before):
    codes = list(bufs)
    width = w_key.shape[1]
    spare = lay.requests

    def last(i, plan):
        start = plan[lay.start + phase]
        count = plan[lay.start + phase + 1] - start
        return jnp.minimum(start + jnp.minimum(i, jnp.maximum(count - 1, 0)), lay.requests - 1)

    def kind(i, plan):
        return plan[lay.kind + last(i, plan)], 0, 0

    def rel(i, plan):
        return plan[lay.rel + last(i, plan)], 0, 0

    def slot(i, plan):
        count = plan[lay.start + phase + 1] - plan[lay.start + phase]
        return jnp.where(i < count, plan[lay.slot + last(i, plan)], spare), 0, 0

    anywhere = pl.BlockSpec(memory_space=pl.ANY)
    weight = pl.BlockSpec((1, width, width), kind)
    piece = pl.BlockSpec((1, hd.rows, 2 * LANES), rel)
    target = pl.BlockSpec((1, TILE, hd.padded), slot)
    shape = jax.ShapeDtypeStruct((spare + lay.slots, TILE, hd.padded), BF16)
    first = 1 + len(codes) + 4
    flops = most * 2 * TILE * 2 * (width * width + hd.rows * 2 * LANES)
    return pl.pallas_call(
        functools.partial(source_body, lay, hd, phase, codes),
        grid_spec=pltpu.PrefetchScalarGridSpec(
            num_scalar_prefetch=1,
            grid=(most,),
            in_specs=[anywhere] * len(codes)
            + [weight, weight, piece, piece]
            + [anywhere] * len(before),
            out_specs=[target, target],
            scratch_shapes=[
                pltpu.VMEM((2, TILE, width), BF16),
                pltpu.SemaphoreType.DMA((2,)),
            ],
        ),
        out_shape=[shape, shape],
        input_output_aliases={first + k: k for k in range(len(before))},
        name="sources",
        **params(cost(flops, most * 2.4e6)),
    )(plan, *bufs.values(), w_key, w_value, p_att, p_msg, *before)


def finish(hd, slots, priors, query, keyed, message, w_out, own, mix, put):
    heads = []
    for head in range(hd.heads):
        at = slice(head * LANES, (head + 1) * LANES)
        q = query[0, :, at]
        scores = []
        for slot in range(slots):
            score = lax.dot_general(
                q, keyed[slot, :, at], (((1,), (1,)), ((), ())), preferred_element_type=F32
            )
            scores.append(score * priors(slot, head))
        scores = jnp.concatenate(scores, axis=1)
        highest = jnp.max(scores, axis=1, keepdims=True)
        exponent = jnp.exp(scores - highest)
        share = 1.0 / jnp.sum(exponent, axis=1, keepdims=True)
        attention = (exponent * share).astype(BF16)
        merged = jnp.dot(
            attention,
            message[:, :, at].reshape(slots * TILE, LANES),
            preferred_element_type=F32,
        )
        active = 0.5 * merged * (1.0 + lax.erf(merged * math.sqrt(0.5)))
        heads.append(active.astype(BF16))
    projected = jnp.dot(
        jnp.concatenate(heads, axis=1), w_out[0], preferred_element_type=F32
    )
    put((mix * projected + (1.0 - mix) * own[0].astype(F32)).astype(BF16))


def prior_of(lay, relation, prior, block, hd):
    def priors(slot, head):
        return prior[relation[block, slot], head] * (1.0 / math.sqrt(hd.size))

    return priors


def offers_body(lay, hd, plan, relation, prior, mix, query, keyed, message, w_out, own, *outs):
    step = pl.program_id(0)
    block = plan[lay.sched + step]

    def put(rows):
        for k, out in enumerate(outs):

            @pl.when(step == k)
            def _(out=out):
                out[...] = rows

    finish(
        hd, lay.slots, prior_of(lay, relation, prior, block, hd), query, keyed, message,
        w_out, own, mix[plan[lay.own_kind + block]], put,
    )


def rest_body(lay, hd, plan, relation, prior, mix, query, keyed, message, w_out, own, *refs):
    offers, out = refs[:-1], refs[-1]
    block = pl.program_id(0)
    offered = plan[lay.offer + block]
    for k, ref in enumerate(offers):

        @pl.when(offered == k)
        def _(ref=ref):
            out[0] = ref[...]

    @pl.when(offered < 0)
    def _():
        def put(rows):
            out[0] = rows

        finish(
            hd, lay.slots, prior_of(lay, relation, prior, block, hd), query, keyed, message,
            w_out, own, mix[plan[lay.own_kind + block]], put,
        )


def attend(lay, hd, plan, relation, prior, mix, query, keyed, message, w_out, blocks, offers):
    width = blocks.shape[2]
    first = offers is None
    smem = pl.BlockSpec(memory_space=pltpu.SMEM)

    def block_at(i, plan):
        return plan[lay.sched + i] if first else i

    def at(i, plan):
        return block_at(i, plan), 0, 0

    def kind(i, plan):
        return plan[lay.own_kind + block_at(i, plan)], 0, 0

    in_specs = [
        smem, smem, smem,
        pl.BlockSpec((1, TILE, hd.padded), at),
        pl.BlockSpec((lay.slots, TILE, hd.padded), at),
        pl.BlockSpec((lay.slots, TILE, hd.padded), at),
        pl.BlockSpec((1, hd.padded, width), kind),
        pl.BlockSpec((1, TILE, width), at),
    ]
    whole = pl.BlockSpec((TILE, width), lambda i, plan: (0, 0))
    one = jax.ShapeDtypeStruct((TILE, width), BF16)
    count = lay.steps if first else lay.nblocks
    work = cost(count * 5e8, count * 3e6, count * hd.heads * lay.slots * TILE * TILE)
    args = (plan, relation, prior, mix, query, keyed, message, w_out, blocks)
    return pl.pallas_call(
        functools.partial(offers_body if first else rest_body, lay, hd),
        grid_spec=pltpu.PrefetchScalarGridSpec(
            num_scalar_prefetch=1,
            grid=(count,),
            in_specs=in_specs if first else in_specs + [whole] * lay.steps,
            out_specs=[whole] * lay.steps if first else pl.BlockSpec((1, TILE, width), at),
        ),
        out_shape=[one] * lay.steps
        if first
        else jax.ShapeDtypeStruct((lay.nblocks, TILE, width), BF16),
        name="offers" if first else "rest",
        **params(work),
    )(*args, *(() if first else offers))


def contrast_body(lay, scale, plan, weights, rows, views, *refs):
    negs, loss, total = refs[: lay.steps], refs[-2], refs[-1]
    block = pl.program_id(0)
    kind = plan[lay.own_kind + block]
    mine = rows[0]
    product = mine.astype(F32) * views[0].astype(F32)
    width = product.shape[1]
    folded = product[:, :LANES]
    for at in range(LANES, width, LANES):
        folded = folded + product[:, at : at + LANES]
    positive = jnp.sum(folded.T, axis=0, keepdims=True) * scale
    logits = []
    for step in range(lay.steps):
        logit = lax.dot_general(
            negs[step][...], mine, (((1,), (1,)), ((), ())), preferred_element_type=F32
        )
        match = plan[lay.neg_kind + step] == kind
        logits.append(jnp.where(match, logit * scale, -jnp.inf))
    highest = positive
    for logit in logits:
        highest = jnp.maximum(highest, jnp.max(logit, axis=0, keepdims=True))
    denominator = jnp.exp(positive - highest)
    for logit in logits:
        denominator = denominator + jnp.sum(jnp.exp(logit - highest), axis=0, keepdims=True)
    result = highest + jnp.log(denominator) - positive
    loss[pl.ds(block, 1), :] = result

    @pl.when(block == 0)
    def _():
        total[...] = jnp.zeros_like(total)

    total[...] += jnp.sum(result, axis=1, keepdims=True) * weights[kind]


def contrast(lay, plan, weights, rows, views, negs):
    width = rows.shape[2]
    at = pl.BlockSpec((1, TILE, width), lambda i, plan: (i, 0, 0))
    whole = pl.BlockSpec((TILE, width), lambda i, plan: (0, 0))
    return pl.pallas_call(
        functools.partial(contrast_body, lay, 1.0 / math.sqrt(width)),
        grid_spec=pltpu.PrefetchScalarGridSpec(
            num_scalar_prefetch=1,
            grid=(lay.nblocks,),
            in_specs=[pl.BlockSpec(memory_space=pltpu.SMEM), at, at] + [whole] * lay.steps,
            out_specs=[
                pl.BlockSpec((lay.nblocks, TILE), lambda i, plan: (0, 0)),
                pl.BlockSpec((1, 1), lambda i, plan: (0, 0)),
            ],
        ),
        out_shape=[
            jax.ShapeDtypeStruct((lay.nblocks, TILE), F32),
            jax.ShapeDtypeStruct((1, 1), F32),
        ],
        name="contrast",
        **params(cost(1e9, 4e6, 5e5)),
    )(plan, weights, rows, views, *negs)


def summed(value, axis):
    count = lax.axis_size(axis)
    if count & (count - 1):
        return lax.psum(value, axis)
    bit = 1
    while bit < count:
        value = value + lax.ppermute(value, axis, [(i, i ^ bit) for i in range(count)])
        bit *= 2
    return value


def shards(
    feats,
    node_type,
    tiles,
    relation,
    neg_sched,
    w_query,
    w_key,
    w_value,
    w_out,
    rel_att,
    rel_msg,
    rel_prior,
    skip_gate,
    pos_view,
    type_weight,
):
    lanes = lax.axis_size("narrow")
    lane = lax.axis_index("narrow")
    width = feats.shape[1]
    nblocks = feats.shape[0] // TILE
    heads, size = rel_att.shape[1], rel_att.shape[2]
    lay = Layout(lanes, nblocks, tiles.shape[1], neg_sched.shape[1], w_query.shape[0])
    hd = Heads(heads, size, width)
    staged = lanes == 8
    blocks = feats.reshape(nblocks, TILE, width)
    cap = lay.cap

    plan = make_plan(
        lay, staged, lane.astype(jnp.int32).reshape(1), tiles, node_type, relation, neg_sched
    )
    p_att, p_msg = spread(hd, rel_att, rel_msg)
    padded_out = jnp.pad(
        w_out.reshape(-1, heads, size, width), ((0, 0), (0, 0), (0, LANES - size), (0, 0))
    ).reshape(-1, hd.padded, width)
    mix = jax.nn.sigmoid(skip_gate)
    query = queries(lay, hd, plan, blocks, w_query, p_att)

    def project(phase, most, bufs, before):
        return sources_of(
            lay, hd, plan, phase, most, bufs, w_key, w_value, p_att, p_msg, before
        )

    if staged:
        deep = lanes // 2

        def moved(array, pairs):
            return lax.ppermute(array, "narrow", pairs)

        ups = [(2 * z + x, 2 * z + 2 + x) for z in range(deep - 1) for x in range(2)]
        downs = [(b, a) for a, b in ups]

        def swaps(depths):
            return [(2 * z + x, 2 * z + 1 - x) for z in depths for x in range(2)]

        def from_first(plan, refs, block, target, sem):
            pltpu.make_async_copy(refs[0].at[block], target, sem).start()

        def from_second(plan, refs, block, target, sem):
            pltpu.make_async_copy(refs[1].at[block], target, sem).start()

        def from_far(plan, refs, block, target, sem):
            low = plan[lay.lane] // 2 < deep // 2

            @pl.when(low)
            def _():
                pltpu.make_async_copy(refs[1].at[block], target, sem).start()

            @pl.when(jnp.logical_not(low))
            def _():
                pltpu.make_async_copy(refs[0].at[block], target, sem).start()

        def own_list(base):
            return lambda plan: base + plan[lay.lane] * cap

        def list_at(offset):
            def base_of(plan):
                other = plan[lay.lane] + 2 * offset
                return lay.partner + jnp.clip(other, 0, lanes - 1) * cap

            return base_of

        def far_list(plan):
            mine = plan[lay.lane]
            return lay.partner + jnp.where(mine // 2 < deep // 2, mine + 4, mine - 4) * cap

        below = moved(blocks, ups)
        above = moved(blocks, downs)
        out_partner, out_ends, out_ends_x = pick(
            lay, plan, [blocks],
            [
                (own_list(lay.partner), from_first),
                (own_list(lay.ends), from_first),
                (own_list(lay.ends_x), from_first),
            ],
        )
        partner = moved(out_partner, swaps(range(deep)))
        relay = moved(out_ends_x, swaps((0, deep - 1)))

        far_below = moved(below, [p for p in ups if 2 <= p[0] < lanes - 2])
        far_above = moved(above, [p for p in downs if 2 <= p[0] < lanes - 2])
        out_below, out_above = pick(
            lay, plan, [below, above],
            [(list_at(-1), from_first), (list_at(1), from_second)],
        )
        below_x = moved(out_below, swaps(range(1, deep)))
        above_x = moved(out_above, swaps(range(deep - 1)))

        (out_far,) = pick(lay, plan, [far_below, far_above], [(far_list, from_far)])
        far_x = moved(out_far, swaps(range(deep)))
        out_ends, relay, far_below, far_above = lax.optimization_barrier(
            (out_ends, relay, far_below, far_above)
        )
        last = lanes - 2
        corners = [(x, last + x) for x in range(2)] + [(last + x, x) for x in range(2)]
        ends = moved(out_ends, corners)
        ends_x = moved(relay, corners)

        made = project(
            0, min(2 * cap + 2 * cap, lay.requests),
            {OWN: blocks, PARTNER: partner, BELOW: below, ABOVE: above}, (),
        )
        made = project(
            1, min(3 * cap, lay.requests),
            {BELOW_X: below_x, ABOVE_X: above_x, FAR_UP: far_below, FAR_DOWN: far_above}, made,
        )
        made = project(2, cap, {FAR_X: far_x}, made)
        made = project(3, min(2 * cap, lay.requests), {ENDS: ends, ENDS_X: ends_x}, made)
    else:
        gathered = lax.all_gather(blocks, "narrow", tiled=True)
        made = project(0, lay.requests, {OWN: gathered}, ())

    keyed, message = made
    shared = (lay, hd, plan, relation, rel_prior, mix, query, keyed, message, padded_out, blocks)
    offers = attend(*shared, None)
    negs = [
        lax.ppermute(
            offers[step], "narrow", [(i, (i + step + 1) % lanes) for i in range(lanes)]
        )
        for step in range(lay.steps)
    ]
    embedding = attend(*shared, offers)
    node_loss, total = contrast(
        lay, plan, type_weight, embedding, pos_view.reshape(nblocks, TILE, width), negs
    )
    total = summed(summed(total, "dom"), "narrow")
    nodes = node_loss.size * lax.axis_size("dom") * lanes
    return (
        embedding.reshape(nblocks * TILE, width),
        node_loss.reshape(nblocks * TILE),
        total[0, 0] / nodes,
    )


def solution(mesh):
    return jax.shard_map(
        shards,
        mesh=mesh,
        in_specs=(
            P(("dom", "narrow"), None),
            P("dom"),
            P("dom", None),
            P(("dom", "narrow"), None),
            P("dom", None),
            P(),
            P(),
            P(),
            P(),
            P(),
            P(),
            P(),
            P(),
            P(("dom", "narrow"), None),
            P(),
        ),
        out_specs=(P(("dom", "narrow"), None), P(("dom", "narrow")), P()),
        check_vma=False,
    )
```

time: 590 us -> 276 us (0.47)
  local copies, waits for them, and re-layouts: 182 us -> 17 us
  Pallas kernels: 0 us -> 164 us
  matrix products: 130 us -> 0 us
  waiting for transfers between devices: 158 us -> 39.9 us
  blocking collectives: 50.8 us -> 0 us
  starting transfers between devices: 12.9 us -> 45.8 us
  loops' own time: 21.4 us -> 0 us
  other arithmetic: 21.1 us -> 0.01 us
    pallas_call x0 -> x13, Pallas kernels: none -> 164 us  [the longest x4 60.5 us: sources_of(): pl.pallas_call(functools.partial(source_body, lay, hd, phase, codes), gri...]
    all_to_all x1 -> x0, waiting for transfers between devices: 146 us -> none  [shards(): lax.all_to_all(outgoing, 'narrow', split_axis=0, concat_axis=0, tiled=True)]
    dot_general x57 -> x0, matrix products: 130 us -> none  [the longest x8 27 us: attend(): jnp.einsum('jmd,jde->jme', src_tiles, w_key[src_types], preferred_element...]
    gather x47 -> x0, local copies, waits for them, and re-layouts: 104 us -> none  [the longest x8 39.8 us: attend(): w_value[src_types]]
    psum x1 -> x0, blocking collectives: 50.8 us -> none  [shards(): overall = lax.psum(jnp.sum(row_weight * node_loss), ('dom', 'narrow'))]
    ppermute x4 -> x20, starting transfers between devices: 6.5 us -> 45.8 us  [the longest x11 26.4 us: moved(): return lax.ppermute(array, 'narrow', pairs)]
    ppermute x4 -> x20, waiting for transfers between devices: 11.5 us -> 39.9 us  [the longest x11 31.4 us: moved(): return lax.ppermute(array, 'narrow', pairs)]
    while x129 -> x0, local copies, waits for them, and re-layouts: 22.8 us -> none
  transfers between devices with their start and end apart: 5 -> 20, of which waited for: 3 -> 6; matrix products, arithmetic and copies ran while one was open for 3% -> 2% of each run, Pallas kernels for 0% -> 50%
where the time goes in v1:
time: 276 us; the launch traced here: 272 us
  Pallas kernels  164 us (59%)
  starting transfers between devices  45.8 us (17%)
  waiting for transfers between devices  39.9 us (14%)
  local copies, waits for them, and re-layouts  17 us (6%)
  between operations  5.52 us (2%)
    pallas_call x4, Pallas kernels, sources_of(): pl.pallas_call(functools.partial(source_body, lay, hd, phase, codes), gri...  60.5 us
    pallas_call x2, Pallas kernels, attend(): pl.pallas_call(functools.partial(offers_body if first else rest_body, lay...  42.4 us
    pallas_call x3, Pallas kernels, pick(): pl.pallas_call(functools.partial(pick_body, [(chooser(b, s), lay.cap) for...  35.8 us
    ppermute x11, waiting for transfers between devices, moved(): return lax.ppermute(array, 'narrow', pairs)  31.4 us
    ppermute x11, starting transfers between devices, moved(): return lax.ppermute(array, 'narrow', pairs)  26.4 us
    unnamed x39, local copies, waits for them, and re-layouts  14.3 us
    ppermute x5, starting transfers between devices, summed(): lax.ppermute(value, axis, [(i, i ^ bit) for i in range(count)])  10.7 us
    ppermute x4, starting transfers between devices, shards(): lax.ppermute(offers[step], 'narrow', [(i, (i + step + 1) % lanes) for i i...  8.74 us
  transfers between devices with their start and end apart: 20, of which 6 were waited for; matrix products, arithmetic and copies ran while one was open for 2% of the time, Pallas kernels for 50%

profile of v1, /device:TPU:12, one launch (start us, length us, event | category | flops | bytes accessed | tf_op | source)
XLA Modules:
  0.0 271.8 jit_solution(8151402039677352388)
XLA Ops:
  0.6 3.5 %collective-permute-start.1 = (bf16[8,128,768]{2,1,0:T(8,128)(2,1)}, bf16[8,128,768]{2,1,0:T(8,128)(2,1)}, u32[]{:S(2)}, u32[]{:S(2)}) collective-permute-start(bf16[8,128,768]{2,1,0:T(8,128)(2,1)} %bitcast.8), channel_id=1, source_target_pairs={{0,2},{1,3},{2,4},{3,5},{4,6},{5,7},{8,10},{9,11},{10,12},{11,13},... | collective-permute-start | bytes 4718600 | tf_op jit(solution)/shard_map/ppermute | solution.py:658
  4.1 3.5 %collective-permute-start.3 = (bf16[8,128,768]{2,1,0:T(8,128)(2,1)}, bf16[8,128,768]{2,1,0:T(8,128)(2,1)}, u32[]{:S(2)}, u32[]{:S(2)}) collective-permute-start(bf16[8,128,768]{2,1,0:T(8,128)(2,1)} %bitcast.9), channel_id=1, source_target_pairs={{2,0},{3,1},{4,2},{5,3},{6,4},{7,5},{10,8},{11,9},{12,10},{13,11},... | collective-permute-start | bytes 4718600 | tf_op jit(solution)/shard_map/ppermute | solution.py:658
  7.6 31.4 %collective-permute-done.1.refs_0_.refs_2_ = bf16[8,128,768]{2,1,0:T(8,128)(2,1)} collective-permute-done((bf16[8,128,768]{2,1,0:T(8,128)(2,1)}, bf16[8,128,768]{2,1,0:T(8,128)(2,1)}, u32[]{:S(2)}, u32[]{:S(2)}) %collective-permute-start.1) | collective-permute-done | bytes 1572896 | tf_op jit(solution)/shard_map/ppermute | solution.py:658
  39.0 3.6 %collective-permute-start.2 = (bf16[8,128,768]{2,1,0:T(8,128)(2,1)}, bf16[8,128,768]{2,1,0:T(8,128)(2,1)S(1)}, u32[]{:S(2)}, u32[]{:S(2)}) collective-permute-start(bf16[8,128,768]{2,1,0:T(8,128)(2,1)} %collective-permute-done.1.refs_0_.refs_2_), channel_id=1, source_target_pairs={{2,4},{3,5},{4,6},{5,7},{10,12},{11,13},{12,14},{13,15},{18,20},{1... | collective-permute-start | bytes 4718600 | tf_op jit(solution)/shard_map/ppermute | solution.py:658
  42.6 3.1 %collective-permute-start.4 = (bf16[8,128,768]{2,1,0:T(8,128)(2,1)}, bf16[8,128,768]{2,1,0:T(8,128)(2,1)S(1)}, u32[]{:S(2)}, u32[]{:S(2)}) collective-permute-start(bf16[8,128,768]{2,1,0:T(8,128)(2,1)} %collective-permute-done.3.refs_1_.refs_3_), channel_id=1, source_target_pairs={{2,0},{3,1},{4,2},{5,3},{10,8},{11,9},{12,10},{13,11},{18,16},{19,... | collective-permute-start | bytes 4718600 | tf_op jit(solution)/shard_map/ppermute | solution.py:658
  45.7 1.3 copy.25.relation
  47.0 1.4 copy.24.tiles
  48.4 1.3 copy.26.sched
  49.8 7.1 %plan.1 = s32[326]{0:T(512)} custom-call(s32[1]{0:T(128)} %bitcast.lane_ref, s32[64,4]{1,0:T(8,128)} %copy.24.tiles, s32[64]{0:T(128)} %kinds.1, s32[8,4]{1,0:T(8,128)} %copy.25.relation, s32[8,4]{1,0:T(8,128)} %copy.26.sched), custom_call_target="tpu_custom_call" | custom-call | flops 100000 | bytes 4096 | tf_op jit(solution)/shard_map/plan/pallas_call | solution.py:200
  56.9 1.4 copy-done.1
  58.3 0.7 copy-done.11
  58.9 2.3 pick.3
  61.2 1.6 collective-permute-start
  62.8 1.5 collective-permute-start.10
  64.3 1.2 copy-done.5
  65.5 1.2 copy-done.6
  66.7 4.4 %spread.1 = (bf16[6,1536,256]{2,1,0:T(8,128)(2,1)}, bf16[6,1536,256]{2,1,0:T(8,128)(2,1)}) custom-call(bf16[5,8,96,96]{3,2,1,0:T(8,128)(2,1)S(1)} %copy-done.5, bf16[5,8,96,96]{3,2,1,0:T(8,128)(2,1)S(1)} %copy-done.6), custom_call_target="tpu_custom_call" | custom-call | flops 1000000 | bytes 9437184 | tf_op jit(solution)/shard_map/spread/pallas_call | solution.py:262
  71.2 31.5 %pick.5 = (bf16[5,128,768]{2,1,0:T(8,128)(2,1)}, bf16[5,128,768]{2,1,0:T(8,128)(2,1)S(1)}) custom-call(s32[326]{0:T(512)S(1)} %copy-done.12, bf16[8,128,768]{2,1,0:T(8,128)(2,1)} %collective-permute-done.1.refs_0_.refs_2_, bf16[8,128,768]{2,1,0:T(8,128)(2,1)} %collective-permute-done.3.refs_1_.refs_3_), custom_call_target="tpu_custom_call" | custom-call | flops 1000 | bytes 3932160 | tf_op jit(solution)/shard_map/pick/pallas_call | solution.py:323
  102.7 2.4 collective-permute-start.8
  105.2 3.4 %collective-permute-start.9 = (bf16[5,128,768]{2,1,0:T(8,128)(2,1)S(1)}, bf16[5,128,768]{2,1,0:T(8,128)(2,1)S(1)}, u32[]{:S(2)}, u32[]{:S(2)}) collective-permute-start(bf16[5,128,768]{2,1,0:T(8,128)(2,1)S(1)} %get-tuple-element.35), channel_id=1, source_target_pairs={{0,1},{1,0},{2,3},{3,2},{4,5},{5,4},{8,9},{9,8},{10,11},{11,10},{1... | collective-permute-start | bytes 2949128 | tf_op jit(solution)/shard_map/ppermute | solution.py:658
  108.6 7.4 %queries.1.query = bf16[8,128,1024]{2,1,0:T(8,128)(2,1)S(1)} custom-call(s32[326]{0:T(512)S(1)} %copy-done.12, bf16[8,128,768]{2,1,0:T(8,128)(2,1)S(1)} %bitcast.11, bf16[3,768,768]{2,1,0:T(8,128)(2,1)} %weight.1, bf16[6,1536,256]{2,1,0:T(8,128)(2,1)} %get-tuple-element.28.pieces.refs_6_.refs_3_.refs_4_), custom_call_target="tpu_custom_call" | custom-call | flops 2000000000 | bytes 10000000 | tf_op jit(solution)/shard_map/queries/pallas_call | solution.py:281
  116.0 2.7 pad.4
  118.7 2.0 pick.4
  121.3 1.6 collective-permute-start.5
  122.9 1.6 collective-permute-start.6
  124.6 28.4 %sources.4 = (bf16[36,128,1024]{2,1,0:T(8,128)(2,1)}, bf16[36,128,1024]{2,1,0:T(8,128)(2,1)}) custom-call(s32[326]{0:T(512)S(1)} %copy-done.12, bf16[8,128,768]{2,1,0:T(8,128)(2,1)S(1)} %bitcast.12, bf16[5,128,768]{2,1,0:T(8,128)(2,1)S(1)} %collective-permute-done.10.refs_1_, bf16[8,128,768]{2,1,0:T(8,128)(2,1)} %collective-permute-done.1.refs_0_.refs_2_, ...), custom_call_target="tpu_custom_call" | custom-call | flops 10066329600 | bytes 48000000 | tf_op jit(solution)/shard_map/sources/pallas_call | solution.py:404
  153.0 0.9 copy-done.7
  153.9 1.0 copy-done.9
  154.9 1.2 copy-done.8
  156.1 1.2 copy-done.10
  157.3 18.4 %sources.5 = (bf16[36,128,1024]{2,1,0:T(8,128)(2,1)}, bf16[36,128,1024]{2,1,0:T(8,128)(2,1)}) custom-call(s32[326]{0:T(512)S(1)} %copy-done.12, bf16[5,128,768]{2,1,0:T(8,128)(2,1)S(1)} %copy-done.8, bf16[5,128,768]{2,1,0:T(8,128)(2,1)S(1)} %copy-done.10, ...), custom_call_target="tpu_custom_call", output_to_operand_aliasing={{0}: (9, {}), {1}: (10, {})} | custom-call | flops 7549747200 | bytes 36000000 | tf_op jit(solution)/shard_map/sources/pallas_call | solution.py:404
  175.8 10.5 %sources.6 = (bf16[36,128,1024]{2,1,0:T(8,128)(2,1)}, bf16[36,128,1024]{2,1,0:T(8,128)(2,1)}) custom-call(s32[326]{0:T(512)S(1)} %copy-done.12, bf16[5,128,768]{2,1,0:T(8,128)(2,1)} %collective-permute-done.7.refs_0_, bf16[3,768,768]{2,1,0:T(8,128)(2,1)S(1)} %copy-done, bf16[3,768,768]{2,1,0:T(8,128)(2,1)} %refs_3_.1, ...), custom_call_target="tpu_custom_call", output_to_operand_aliasing={{0}: (6, {}), {1}: (7, {})} | custom-call | flops 2516582400 | bytes 12000000 | tf_op jit(solution)/shard_map/sources/pallas_call | solution.py:404
  186.3 3.2 %sources.7 = (bf16[36,128,1024]{2,1,0:T(8,128)(2,1)}, bf16[36,128,1024]{2,1,0:T(8,128)(2,1)}) custom-call(s32[326]{0:T(512)S(1)} %copy-done.12, bf16[5,128,768]{2,1,0:T(8,128)(2,1)} %collective-permute-done.5.refs_0_, bf16[5,128,768]{2,1,0:T(8,128)(2,1)} %collective-permute-done.6.refs_1_, ...), custom_call_target="tpu_custom_call", output_to_operand_aliasing={{0}: (7, {}), {1}: (8, {})} | custom-call | flops 5033164800 | bytes 24000000 | tf_op jit(solution)/shard_map/sources/pallas_call | solution.py:404
  189.5 17.3 %offers.1 = (bf16[128,768]{1,0:T(8,128)(2,1)S(1)}, bf16[128,768]{1,0:T(8,128)(2,1)S(1)}, bf16[128,768]{1,0:T(8,128)(2,1)S(1)}, bf16[128,768]{1,0:T(8,128)(2,1)S(1)}) custom-call(s32[326]{0:T(512)S(1)} %copy-done.12, s32[8,4]{1,0:T(8,128)S(1)} %copy-done.13, f32[5,8]{1,0:T(8,128)S(1)} %copy-done.14, f32[3]{0:T(128)S(1)} %add_divide_fusion.mix, ...), custom_call_target="tpu_custom_call" | custom-call | flops 2000000000 | bytes 12000000 | tf_op jit(solution)/shard_map/offers/pallas_call | solution.py:526
  206.8 1.5 collective-permute-start.11
  208.3 1.0 collective-permute-start.12
  209.3 5.7 %collective-permute-start.13 = (bf16[128,768]{1,0:T(8,128)(2,1)S(1)}, bf16[128,768]{1,0:T(8,128)(2,1)S(1)}, u32[]{:S(2)}, u32[]{:S(2)}) collective-permute-start(bf16[128,768]{1,0:T(8,128)(2,1)S(1)} %get-tuple-element.49.refs_2_), channel_id=1, source_target_pairs={{0,3},{1,4},{2,5},{3,6},{4,7},{5,0},{6,1},{7,2},{8,11},{9,12},{10,... | collective-permute-start | bytes 589832 | tf_op jit(solution)/shard_map/ppermute | solution.py:747
  215.6 25.1 %rest.1.rows = bf16[8,128,768]{2,1,0:T(8,128)(2,1)} custom-call(s32[326]{0:T(512)S(1)} %copy-done.12, s32[8,4]{1,0:T(8,128)S(1)} %copy-done.13, f32[5,8]{1,0:T(8,128)S(1)} %copy-done.14, f32[3]{0:T(128)S(1)} %add_divide_fusion.mix, bf16[8,128,1024]{2,1,0:T(8,128)(2,1)S(1)} %queries.1.query, bf16[36,128,1024]{2,1,0:T(8,128)(2,1)} %get-tuple-element.45.keyed, ...), custom_call_target="tpu_custom_call" | custom-call | flops 4000000000 | bytes 24000000 | tf_op jit(solution)/shard_map/rest/pallas_call | solution.py:526
  240.7 1.4 copy-done.3
  242.1 6.0 %contrast.1 = (f32[8,128]{1,0:T(8,128)}, f32[1,1]{1,0:T(1,128)}) custom-call(s32[326]{0:T(512)S(1)} %copy-done.12, f32[3]{0:T(128)S(1)} %copy-done.15, bf16[8,128,768]{2,1,0:T(8,128)(2,1)S(1)} %copy-done.3, bf16[8,128,768]{2,1,0:T(8,128)(2,1)S(1)} %bitcast.16, bf16[128,768]{1,0:T(8,128)(2,1)S(1)} %collective-permute-done.11.refs_0_, ...), custom_call_target="tpu_custom_call" | custom-call | flops 1000000000 | bytes 4000000 | tf_op jit(solution)/shard_map/contrast/pallas_call | solution.py:580
  248.1 1.4 collective-permute-done.15
  250.7 5.4 %collective-permute-start.16 = (f32[1,1]{1,0:T(1,128)}, f32[1,1]{1,0:T(1,128)}, u32[]{:S(2)}, u32[]{:S(2)}) collective-permute-start(f32[1,1]{1,0:T(1,128)} %add.21), channel_id=1, source_target_pairs={{0,16},{8,24},{16,0},{24,8},{1,17},{9,25},{17,1},{25,9},{2,18},{10... | collective-permute-start | bytes 20 | tf_op jit(solution)/shard_map/ppermute | solution.py:606
  257.0 1.4 collective-permute-start.17
  258.4 2.3 collective-permute-done.17
  261.3 1.4 collective-permute-start.18
  262.6 2.3 collective-permute-done.18
  265.5 2.5 collective-permute-start.19
  268.0 2.1 collective-permute-done.19
  (46 shorter events, 1.6 us)
Async XLA Ops:
  0.6 70.5 %copy-start.17 = (f32[3]{0:T(128)S(1)}, f32[3]{0:T(128)}, u32[]{:S(2)}) copy-start(f32[3]{0:T(128)} %param.27) | copy-start | bytes 40
  0.6 38.3 %collective-permute-start.1 = (bf16[8,128,768]{2,1,0:T(8,128)(2,1)}, bf16[8,128,768]{2,1,0:T(8,128)(2,1)}, u32[]{:S(2)}, u32[]{:S(2)}) collective-permute-start(bf16[8,128,768]{2,1,0:T(8,128)(2,1)} %bitcast.8), channel_id=1, source_target_pairs={{0,2},{1,3},{2,4},{3,5},{4,6},{5,7},{8,10},{9,11},{10,12},{11,13},... | collective-permute-start | bytes 4718600 | tf_op jit(solution)/shard_map/ppermute | solution.py:658
  4.1 38.4 %collective-permute-start.3 = (bf16[8,128,768]{2,1,0:T(8,128)(2,1)}, bf16[8,128,768]{2,1,0:T(8,128)(2,1)}, u32[]{:S(2)}, u32[]{:S(2)}) collective-permute-start(bf16[8,128,768]{2,1,0:T(8,128)(2,1)} %bitcast.9), channel_id=1, source_target_pairs={{2,0},{3,1},{4,2},{5,3},{6,4},{7,5},{10,8},{11,9},{12,10},{13,11},... | collective-permute-start | bytes 4718600 | tf_op jit(solution)/shard_map/ppermute | solution.py:658
  39.0 66.2 %collective-permute-start.2 = (bf16[8,128,768]{2,1,0:T(8,128)(2,1)}, bf16[8,128,768]{2,1,0:T(8,128)(2,1)S(1)}, u32[]{:S(2)}, u32[]{:S(2)}) collective-permute-start(bf16[8,128,768]{2,1,0:T(8,128)(2,1)} %collective-permute-done.1.refs_0_.refs_2_), channel_id=1, source_target_pairs={{2,4},{3,5},{4,6},{5,7},{10,12},{11,13},{12,14},{13,15},{18,20},{1... | collective-permute-start | bytes 4718600 | tf_op jit(solution)/shard_map/ppermute | solution.py:658
  42.6 76.1 %collective-permute-start.4 = (bf16[8,128,768]{2,1,0:T(8,128)(2,1)}, bf16[8,128,768]{2,1,0:T(8,128)(2,1)S(1)}, u32[]{:S(2)}, u32[]{:S(2)}) collective-permute-start(bf16[8,128,768]{2,1,0:T(8,128)(2,1)} %collective-permute-done.3.refs_1_.refs_3_), channel_id=1, source_target_pairs={{2,0},{3,1},{4,2},{5,3},{10,8},{11,9},{12,10},{13,11},{18,16},{19,... | collective-permute-start | bytes 4718600 | tf_op jit(solution)/shard_map/ppermute | solution.py:658
  56.8 1.4 copy-start.1
  58.3 0.7 copy-start.11
  58.9 12.3 %copy-start.12 = (s32[326]{0:T(512)S(1)}, s32[326]{0:T(512)}, u32[]{:S(2)}) copy-start(s32[326]{0:T(512)} %plan.1) | copy-start | bytes 3916
  58.9 49.7 %copy-start.2 = (bf16[1024,768]{1,0:T(8,128)(2,1)S(1)}, bf16[1024,768]{1,0:T(8,128)(2,1)}, u32[]{:S(2)}) copy-start(bf16[1024,768]{1,0:T(8,128)(2,1)} %param.15) | copy-start | bytes 4718596
  61.2 59.5 %collective-permute-start = (bf16[5,128,768]{2,1,0:T(8,128)(2,1)}, bf16[5,128,768]{2,1,0:T(8,128)(2,1)}, u32[]{:S(2)}, u32[]{:S(2)}) collective-permute-start(bf16[5,128,768]{2,1,0:T(8,128)(2,1)} %get-tuple-element.30), channel_id=1, source_target_pairs={{0,1},{1,0},{6,7},{7,6},{8,9},{9,8},{14,15},{15,14},{16,17},{17,16... | collective-permute-start | bytes 2949128 | tf_op jit(solution)/shard_map/ppermute | solution.py:658
  62.8 60.1 %collective-permute-start.10 = (bf16[5,128,768]{2,1,0:T(8,128)(2,1)}, bf16[5,128,768]{2,1,0:T(8,128)(2,1)S(1)}, u32[]{:S(2)}, u32[]{:S(2)}) collective-permute-start(bf16[5,128,768]{2,1,0:T(8,128)(2,1)} %get-tuple-element.38), channel_id=1, source_target_pairs={{0,1},{1,0},{2,3},{3,2},{4,5},{5,4},{6,7},{7,6},{8,9},{9,8},{10,11... | collective-permute-start | bytes 2949128 | tf_op jit(solution)/shard_map/ppermute | solution.py:658
  64.3 1.2 copy-start.5
  65.5 1.2 copy-start.6
  102.7 50.2 %collective-permute-start.8 = (bf16[5,128,768]{2,1,0:T(8,128)(2,1)}, bf16[5,128,768]{2,1,0:T(8,128)(2,1)S(1)}, u32[]{:S(2)}, u32[]{:S(2)}) collective-permute-start(bf16[5,128,768]{2,1,0:T(8,128)(2,1)} %get-tuple-element.34), channel_id=1, source_target_pairs={{2,3},{3,2},{4,5},{5,4},{6,7},{7,6},{10,11},{11,10},{12,13},{13,12... | collective-permute-start | bytes 2949128 | tf_op jit(solution)/shard_map/ppermute | solution.py:658
  105.2 48.7 %collective-permute-start.9 = (bf16[5,128,768]{2,1,0:T(8,128)(2,1)S(1)}, bf16[5,128,768]{2,1,0:T(8,128)(2,1)S(1)}, u32[]{:S(2)}, u32[]{:S(2)}) collective-permute-start(bf16[5,128,768]{2,1,0:T(8,128)(2,1)S(1)} %get-tuple-element.35), channel_id=1, source_target_pairs={{0,1},{1,0},{2,3},{3,2},{4,5},{5,4},{8,9},{9,8},{10,11},{11,10},{1... | collective-permute-start | bytes 2949128 | tf_op jit(solution)/shard_map/ppermute | solution.py:658
  108.6 7.4 %copy-start.16 = (bf16[3,768,768]{2,1,0:T(8,128)(2,1)S(1)}, bf16[3,768,768]{2,1,0:T(8,128)(2,1)}, u32[]{:S(2)}) copy-start(bf16[3,768,768]{2,1,0:T(8,128)(2,1)} %param.23) | copy-start | bytes 10616836
  120.7 55.0 %collective-permute-start.7 = (bf16[5,128,768]{2,1,0:T(8,128)(2,1)S(1)}, bf16[5,128,768]{2,1,0:T(8,128)(2,1)}, u32[]{:S(2)}, u32[]{:S(2)}) collective-permute-start(bf16[5,128,768]{2,1,0:T(8,128)(2,1)S(1)} %pick.4), channel_id=1, source_target_pairs={{0,1},{1,0},{2,3},{3,2},{4,5},{5,4},{6,7},{7,6},{8,9},{9,8},{10,11... | collective-permute-start | bytes 2949128 | tf_op jit(solution)/shard_map/ppermute | solution.py:658
  121.3 65.0 %collective-permute-start.5 = (bf16[5,128,768]{2,1,0:T(8,128)(2,1)}, bf16[5,128,768]{2,1,0:T(8,128)(2,1)}, u32[]{:S(2)}, u32[]{:S(2)}) collective-permute-start(bf16[5,128,768]{2,1,0:T(8,128)(2,1)} %get-tuple-element.31), channel_id=1, source_target_pairs={{0,6},{1,7},{6,0},{7,1},{8,14},{9,15},{14,8},{15,9},{16,22},{17,23... | collective-permute-start | bytes 2949128 | tf_op jit(solution)/shard_map/ppermute | solution.py:658
  122.9 63.4 %collective-permute-start.6 = (bf16[5,128,768]{2,1,0:T(8,128)(2,1)}, bf16[5,128,768]{2,1,0:T(8,128)(2,1)}, u32[]{:S(2)}, u32[]{:S(2)}) collective-permute-start(bf16[5,128,768]{2,1,0:T(8,128)(2,1)} %collective-permute-done), channel_id=1, source_target_pairs={{0,6},{1,7},{6,0},{7,1},{8,14},{9,15},{14,8},{15,9},{16,22},{17,23... | collective-permute-start | bytes 2949128 | tf_op jit(solution)/shard_map/ppermute | solution.py:658
  153.0 0.9 copy-start.7
  153.9 1.0 copy-start.9
  154.9 1.2 copy-start.8
  156.1 1.2 copy-start.10
  157.3 18.4 %copy-start = (bf16[3,768,768]{2,1,0:T(8,128)(2,1)S(1)}, bf16[3,768,768]{2,1,0:T(8,128)(2,1)}, u32[]{:S(2)}) copy-start(bf16[3,768,768]{2,1,0:T(8,128)(2,1)} %refs_2_.3) | copy-start | bytes 10616836
  186.3 3.2 %copy-start.13 = (s32[8,4]{1,0:T(8,128)S(1)}, s32[8,4]{1,0:T(8,128)}, u32[]{:S(2)}) copy-start(s32[8,4]{1,0:T(8,128)} %copy.25.relation) | copy-start | bytes 388
  186.3 3.2 %copy-start.14 = (f32[5,8]{1,0:T(8,128)S(1)}, f32[5,8]{1,0:T(8,128)}, u32[]{:S(2)}) copy-start(f32[5,8]{1,0:T(8,128)} %prior.3) | copy-start | bytes 484
  206.8 33.8 %collective-permute-start.11 = (bf16[128,768]{1,0:T(8,128)(2,1)S(1)}, bf16[128,768]{1,0:T(8,128)(2,1)S(1)}, u32[]{:S(2)}, u32[]{:S(2)}) collective-permute-start(bf16[128,768]{1,0:T(8,128)(2,1)S(1)} %get-tuple-element.47.refs_0_), channel_id=1, source_target_pairs={{0,1},{1,2},{2,3},{3,4},{4,5},{5,6},{6,7},{7,0},{8,9},{9,10},{10,1... | collective-permute-start | bytes 589832 | tf_op jit(solution)/shard_map/ppermute | solution.py:747
  208.3 32.3 %collective-permute-start.12 = (bf16[128,768]{1,0:T(8,128)(2,1)S(1)}, bf16[128,768]{1,0:T(8,128)(2,1)S(1)}, u32[]{:S(2)}, u32[]{:S(2)}) collective-permute-start(bf16[128,768]{1,0:T(8,128)(2,1)S(1)} %get-tuple-element.48.refs_1_), channel_id=1, source_target_pairs={{0,2},{1,3},{2,4},{3,5},{4,6},{5,7},{6,0},{7,1},{8,10},{9,11},{10,... | collective-permute-start | bytes 589832 | tf_op jit(solution)/shard_map/ppermute | solution.py:747
  209.3 31.4 %collective-permute-start.13 = (bf16[128,768]{1,0:T(8,128)(2,1)S(1)}, bf16[128,768]{1,0:T(8,128)(2,1)S(1)}, u32[]{:S(2)}, u32[]{:S(2)}) collective-permute-start(bf16[128,768]{1,0:T(8,128)(2,1)S(1)} %get-tuple-element.49.refs_2_), channel_id=1, source_target_pairs={{0,3},{1,4},{2,5},{3,6},{4,7},{5,0},{6,1},{7,2},{8,11},{9,12},{10,... | collective-permute-start | bytes 589832 | tf_op jit(solution)/shard_map/ppermute | solution.py:747
  215.0 25.7 %copy-start.4 = (bf16[1024,768]{1,0:T(8,128)(2,1)S(1)}, bf16[1024,768]{1,0:T(8,128)(2,1)}, u32[]{:S(2)}) copy-start(bf16[1024,768]{1,0:T(8,128)(2,1)} %param.28) | copy-start | bytes 4718596
  215.0 25.7 %copy-start.15 = (f32[3]{0:T(128)S(1)}, f32[3]{0:T(128)}, u32[]{:S(2)}) copy-start(f32[3]{0:T(128)} %weights.1) | copy-start | bytes 40
  215.0 25.7 %collective-permute-start.14 = (bf16[128,768]{1,0:T(8,128)(2,1)S(1)}, bf16[128,768]{1,0:T(8,128)(2,1)S(1)}, u32[]{:S(2)}, u32[]{:S(2)}) collective-permute-start(bf16[128,768]{1,0:T(8,128)(2,1)S(1)} %get-tuple-element.50.refs_3_), channel_id=1, source_target_pairs={{0,4},{1,5},{2,6},{3,7},{4,0},{5,1},{6,2},{7,3},{8,12},{9,13},{10,... | collective-permute-start | bytes 589832 | tf_op jit(solution)/shard_map/ppermute | solution.py:747
  240.7 1.4 copy-start.3
  248.1 1.4 collective-permute-start.15
  250.7 5.7 %collective-permute-start.16 = (f32[1,1]{1,0:T(1,128)}, f32[1,1]{1,0:T(1,128)}, u32[]{:S(2)}, u32[]{:S(2)}) collective-permute-start(f32[1,1]{1,0:T(1,128)} %add.21), channel_id=1, source_target_pairs={{0,16},{8,24},{16,0},{24,8},{1,17},{9,25},{17,1},{25,9},{2,18},{10... | collective-permute-start | bytes 20 | tf_op jit(solution)/shard_map/ppermute | solution.py:606
  257.0 3.7 %collective-permute-start.17 = (f32[1,1]{1,0:T(1,128)}, f32[1,1]{1,0:T(1,128)}, u32[]{:S(2)}, u32[]{:S(2)}) collective-permute-start(f32[1,1]{1,0:T(1,128)} %add.22), channel_id=1, source_target_pairs={{0,1},{1,0},{2,3},{3,2},{4,5},{5,4},{6,7},{7,6},{8,9},{9,8},{10,11... | collective-permute-start | bytes 20 | tf_op jit(solution)/shard_map/ppermute | solution.py:606
  261.3 3.7 %collective-permute-start.18 = (f32[1,1]{1,0:T(1,128)}, f32[1,1]{1,0:T(1,128)}, u32[]{:S(2)}, u32[]{:S(2)}) collective-permute-start(f32[1,1]{1,0:T(1,128)} %add.23), channel_id=1, source_target_pairs={{0,2},{1,3},{2,0},{3,1},{4,6},{5,7},{6,4},{7,5},{8,10},{9,11},{10,... | collective-permute-start | bytes 20 | tf_op jit(solution)/shard_map/ppermute | solution.py:606
  265.5 4.6 %collective-permute-start.19 = (f32[1,1]{1,0:T(1,128)}, f32[1,1]{1,0:T(1,128)}, u32[]{:S(2)}, u32[]{:S(2)}) collective-permute-start(f32[1,1]{1,0:T(1,128)} %add.24), channel_id=1, source_target_pairs={{0,4},{1,5},{2,6},{3,7},{4,0},{5,1},{6,2},{7,3},{8,12},{9,13},{10,... | collective-permute-start | bytes 20 | tf_op jit(solution)/shard_map/ppermute | solution.py:606
